TPU v7x, 32 devices: a whole 2x2x4 slice. The times are simulated.
32 devices in a mesh: gx: 4 (over x, core), gy: 8 (over z, y).
Axes of the slice: x: 2, y: 2, z: 4, core: 2. Of those that a mesh axis runs over, the one named last changes fastest.
Arguments:
- old_heads: float32 [4, 512, 1024], P(None, 'gx', 'gy'), may hold values from -6 to 6
- conductance_x: float32 [4, 512, 1024], P(None, 'gx', 'gy'), may hold values from 7.6 to 10.4
- conductance_y: float32 [4, 512, 1024], P(None, 'gx', 'gy'), may hold values from 7.6 to 10.4
- storage: float32 [4, 512, 1024], P(None, 'gx', 'gy'), may hold values from 0.25 to 4
- sources: float32 [4, 512, 1024], P(None, 'gx', 'gy'), may hold values from -6 to 6
- cotangent: float32 [4, 512, 1024], P(None, 'gx', 'gy'), may hold values from -6 to 6
- active_mask: int32 [512, 1024], P('gx', 'gy'), may hold values from 0 to 1, as said below
- layer_scale: float32 [64], replicated, may hold values from 0.5 to 2
- window_layers: int32 [4], replicated, may hold values from 0 to 63
Outputs:
- new_heads: float32 [4, 512, 1024], P(None, 'gx', 'gy')
- grad_heads: float32 [4, 512, 1024], P(None, 'gx', 'gy')
- sensitivity_x: float32 [4, 512, 1024], P(None, 'gx', 'gy')
- sensitivity_y: float32 [4, 512, 1024], P(None, 'gx', 'gy')
Inputs may be any that keep to these rules, and one draw needn't show every extreme that they name: `active_mask`: 1 for an active column of cells, 0 for an inactive one.
All inputs are finite; a program needn't handle non-finite values.
Results may differ from a plain program's by a relative error of at most 0.0017.
Values sent between devices are 32-bit elements; how exact they have to be, the bound alone decides.
A program may use at most 128 MiB of HBM per device.

v0:
```python
import functools

import jax
import jax.numpy as jnp
from jax import lax
from jax.experimental import pallas as pl
from jax.experimental.pallas import tpu as pltpu
from jax.sharding import PartitionSpec as P

MESH = pl.DeviceIdType.MESH
BLOCKS = 8
SHIFTS = (1, 2, 4)
G1, G2, T, R1, R2, F, A = range(7)


def schedule(length):
    alive = list(range(length))
    order = []
    while len(alive) > 2:
        gone = alive[1:-1:2]
        for node in gone:
            at = alive.index(node)
            order.append((node, alive[at - 1], alive[at + 1]))
        alive = [node for node in alive if node not in gone]
    return order


def weights(fl, fr, s):
    inv = 1.0 / (fl + fr + s)
    return fl * inv, fr * inv, inv


def merge(a, b, face):
    g1, g2, t = a
    bg1, bg2, bt = b
    wla, wra, ia = weights(t, face, g2)
    through = t * wra
    gb = bg1 + wra * g2
    wlb, wrb, ib = weights(through, bt, gb)
    return (g1 + wla * g2 + wlb * gb, bg2 + wrb * gb, through * wrb), (wla, wra, ia, wlb, wrb, ib)


def merge_right(a, b, coef):
    wla, wra, ia, wlb, wrb, ib = coef
    r1, r2 = a
    rb = b[0] + wra * r2
    return (r1 + wla * r2 + wlb * rb, b[1] + wrb * rb), (r2 * ia, rb * ib)


def split(x1, x2, coef, parts):
    wla, wra, _, wlb, wrb, _ = coef
    b1 = wlb * x1 + wrb * x2 + parts[1]
    a2 = wla * x1 + wra * b1 + parts[0]
    return a2, b1


def roll(value, shift):
    return pltpu.roll(value, shift % BLOCKS, 1)


def sub_index(shape):
    return lax.broadcasted_iota(jnp.int32, shape, 1)


def slab(ref, k, step):
    return ref[:, pl.ds(k, BLOCKS, stride=step), :]


def put_slab(ref, k, step, value):
    ref[:, pl.ds(k, BLOCKS, stride=step), :] = value


class Direction:
    def __init__(self, axis, count, length, layers, refs):
        self.axis, self.count, self.step, self.layers = axis, count, length // BLOCKS, layers
        (self.coef, self.part, self.face, self.flux, self.bcoef, self.bpart, self.dcoef, self.dx, self.ends,
         self.buf_a, self.buf_b, self.send_a, self.recv_a, self.send_b, self.recv_b) = refs
        self.me = lax.axis_index(axis)
        self.order = schedule(self.step)

    def peer(self, offset):
        return lax.rem(self.me + offset, self.count)

    def greet(self, barrier):
        for offset in range(1, self.count):
            pl.semaphore_signal(barrier, inc=1, device_id={self.axis: self.peer(offset)}, device_id_type=MESH)

    def copies(self, buf, send, recv):
        return [
            pltpu.make_async_remote_copy(
                src_ref=buf.at[self.me],
                dst_ref=buf.at[self.me],
                send_sem=send.at[offset - 1],
                recv_sem=recv.at[offset - 1],
                device_id={self.axis: self.peer(offset)},
                device_id_type=MESH,
            )
            for offset in range(1, self.count)
        ]

    def reduce_right(self, right, phase):
        for i, l, r in self.order:
            wl, wr, inv = self.coef[i, 0], self.coef[i, 1], self.coef[i, 2]
            right[l] = right[l] + wl * right[i]
            right[r] = right[r] + wr * right[i]
            self.part[phase, i] = right[i] * inv
        pair = (right[0], right[-1])
        for level, shift in enumerate(SHIFTS):
            coef = [self.bcoef[level, c] for c in range(6)]
            pair, parts = merge_right(pair, [roll(v, -shift) for v in pair], coef)
            self.bpart[phase, level, 0], self.bpart[phase, level, 1] = parts
        return pair

    def post(self, buf, at, value, sub=0):
        for layer in range(self.layers):
            buf[self.me, pl.ds(at * self.layers + layer, 1), :] = value[layer, sub : sub + 1, :]

    def begin_a(self, cond, storage, active, weight, right_of):
        step = self.step
        act = [active[pl.ds(k, BLOCKS, stride=step), :] for k in range(step)]
        weight = weight[...]
        store = [slab(storage, k, step) for k in range(step)]
        right = [right_of(k) for k in range(step)]
        face = []
        for k in range(step):
            raw = jnp.exp(slab(cond, k, step)) * weight * act[k][None]
            if k == step - 1:
                self.post(self.buf_a, F, raw, BLOCKS - 1)
                after = pltpu.roll(act[0], BLOCKS - 1, 0)
            else:
                after = act[k + 1]
            face.append(raw * after[None])
            self.face[k] = face[k]
        for i, l, r in self.order:
            wl, wr, inv = weights(face[l], face[i], store[i])
            store[l] = store[l] + wl * store[i]
            store[r] = store[r] + wr * store[i]
            face[l] = face[l] * wr
            self.coef[i, 0], self.coef[i, 1], self.coef[i, 2] = wl, wr, inv
        seg, link = (store[0], store[-1], face[0]), face[-1]
        for level, shift in enumerate(SHIFTS):
            seg, coef = merge(seg, [roll(v, -shift) for v in seg], link)
            link = roll(link, -shift)
            for c in range(6):
                self.bcoef[level, c] = coef[c]
        pair = self.reduce_right(right, 0)
        for at, value in ((G1, seg[0]), (G2, seg[1]), (T, seg[2]), (R1, pair[0]), (R2, pair[1])):
            self.post(self.buf_a, at, value)
        rows = self.layers * A
        self.buf_a[self.me, pl.ds(rows, 8), :] = jnp.broadcast_to(act[0][0:1], (8, act[0].shape[1]))

    def begin_b(self, right_of):
        pair = self.reduce_right([right_of(k) for k in range(self.step)], 1)
        self.post(self.buf_b, 0, pair[0])
        self.post(self.buf_b, 1, pair[1])

    def dev(self, d, at):
        return self.buf_a[d, pl.ds(at * self.layers, self.layers), :]

    def factor_devices(self):
        first_act = [self.buf_a[d, pl.ds(self.layers * A, 1), :] for d in range(self.count)]
        segs = [tuple(self.dev(d, q) for q in (G1, G2, T)) for d in range(self.count)]
        faces = [self.dev(d, F) * first_act[d + 1] for d in range(self.count - 1)] + [jnp.zeros_like(segs[0][0])]
        for d in range(self.count):
            self.ends[d, pl.ds(0, self.layers), :] = faces[d]
        slot = 0
        while len(segs) > 1:
            joined, links = [], []
            for at in range(0, len(segs) - 1, 2):
                seg, coef = merge(segs[at], segs[at + 1], faces[at])
                for c in range(6):
                    self.dcoef[slot, c] = coef[c]
                slot += 1
                joined.append(seg)
                links.append(faces[at + 1])
            if len(segs) % 2:
                joined.append(segs[-1])
                links.append(faces[-1])
            segs, faces = joined, links
        g1, g2, t = segs[0]
        inv = 1.0 / (t + g2)
        w = t * inv
        self.dcoef[slot, 0], self.dcoef[slot, 1], self.dcoef[slot, 2] = w, inv, 1.0 / (g1 + w * g2)

    def solve_devices(self, pairs):
        slot, tree = 0, []
        while len(pairs) > 1:
            joined, record = [], []
            for at in range(0, len(pairs) - 1, 2):
                coef = [self.dcoef[slot, c] for c in range(6)]
                pair, parts = merge_right(pairs[at], pairs[at + 1], coef)
                slot += 1
                joined.append(pair)
                record.append((coef, parts))
            if len(pairs) % 2:
                joined.append(pairs[-1])
                record.append(None)
            pairs = joined
            tree.append(record)
        r1, r2 = pairs[0]
        w, inv, top = (self.dcoef[slot, c] for c in range(3))
        x1 = (r1 + w * r2) * top
        found = [(x1, w * x1 + r2 * inv)]
        for record in reversed(tree):
            lower = []
            for (x1, x2), entry in zip(found, record):
                if entry is None:
                    lower.append((x1, x2))
                else:
                    a2, b1 = split(x1, x2, *entry)
                    lower += [(x1, a2), (b1, x2)]
            found = lower
        for d, (x1, x2) in enumerate(found):
            self.dx[d, pl.ds(0, self.layers), :] = x1
            self.dx[d, pl.ds(self.layers, self.layers), :] = x2

    def wide(self, ref, index, row):
        rows = [ref[index, pl.ds(row + layer, 1), :] for layer in range(self.layers)]
        return jnp.stack([jnp.broadcast_to(v, (BLOCKS, v.shape[1])) for v in rows])

    def expand(self, phase):
        first, last = self.wide(self.dx, self.me, 0), self.wide(self.dx, self.me, self.layers)
        beyond = self.wide(self.dx, jnp.minimum(self.me + 1, self.count - 1), 0)
        block = sub_index(first.shape)
        for level in reversed(range(len(SHIFTS))):
            shift = SHIFTS[level]
            coef = [self.bcoef[level, c] for c in range(6)]
            a2, b1 = split(first, last, coef, (self.bpart[phase, level, 0], self.bpart[phase, level, 1]))
            odd = lax.rem(block, 2 * shift) == shift
            first = jnp.where(odd, roll(b1, shift), first)
            last = jnp.where(odd, roll(last, shift), a2)
        x = [None] * self.step
        x[0], x[-1] = first, last
        for i, l, r in reversed(self.order):
            x[i] = self.coef[i, 0] * x[l] + self.coef[i, 1] * x[r] + self.part[phase, i]
        after = x[1:] + [jnp.where(block == BLOCKS - 1, beyond, roll(x[0], -1))]
        return x, [now - then for now, then in zip(x, after)]

    def end_a(self):
        self.factor_devices()
        self.solve_devices([(self.dev(d, R1), self.dev(d, R2)) for d in range(self.count)])
        x, change = self.expand(0)
        for k in range(self.step):
            face = self.face[k]
            if k == self.step - 1:
                face = jnp.where(sub_index(face.shape) == BLOCKS - 1, self.wide(self.ends, self.me, 0), face)
            self.flux[k] = -face * change[k]
        return x

    def end_b(self):
        n = self.layers
        self.solve_devices([(self.buf_b[d, pl.ds(0, n), :], self.buf_b[d, pl.ds(n, n), :]) for d in range(self.count)])
        x, change = self.expand(1)
        return x, [self.flux[k] * change[k] for k in range(self.step)]


def kernel(counts, heads, cond_x, cond_y, storage, sources, cotangent, mask, scale, window,
           new_heads, grad_heads, sens_x, sens_y,
           weight, act, act_t, cond_t, store_t, work, work_t, other_t, *rest):
    layers, rows, columns = heads.shape
    half = len(rest) // 2
    x = Direction("gx", counts[0], rows, layers, rest[:half])
    y = Direction("gy", counts[1], columns, layers, rest[half:])
    barrier = pltpu.get_barrier_semaphore()
    x.greet(barrier)
    y.greet(barrier)

    for layer in range(layers):
        weight[layer] = jnp.full(weight.shape[1:], scale[window[layer]], jnp.float32)
    act[...] = mask[...].astype(jnp.float32)
    act_t[...] = act[...].T
    for layer in range(layers):
        cond_t[layer] = cond_y[layer].T
        store_t[layer] = storage[layer].T
        work_t[layer] = cotangent[layer].T

    y.begin_a(cond_t, store_t, act_t, weight, lambda k: slab(work_t, k, y.step))
    pl.semaphore_wait(barrier, counts[0] + counts[1] - 2)
    y_a = y.copies(y.buf_a, y.send_a, y.recv_a)
    for copy in y_a:
        copy.start()

    x.begin_a(cond_x, storage, act, weight,
              lambda k: slab(storage, k, x.step) * slab(heads, k, x.step) + slab(sources, k, x.step))
    x_a = x.copies(x.buf_a, x.send_a, x.recv_a)
    for copy in x_a:
        copy.start()

    for copy in x_a:
        copy.wait()
    for k, value in enumerate(x.end_a()):
        put_slab(work, k, x.step, slab(storage, k, x.step) * value)
    for layer in range(layers):
        work_t[layer] = work[layer].T
    y.begin_b(lambda k: slab(work_t, k, y.step))

    for copy in y_a:
        copy.wait()
    y_b = y.copies(y.buf_b, y.send_b, y.recv_b)
    for copy in y_b:
        copy.start()
    for k, value in enumerate(y.end_a()):
        put_slab(other_t, k, y.step, slab(store_t, k, y.step) * value)
    for layer in range(layers):
        work[layer] = other_t[layer].T
    x.begin_b(lambda k: slab(work, k, x.step))
    x_b = x.copies(x.buf_b, x.send_b, x.recv_b)
    for copy in x_b:
        copy.start()

    for copy in y_b:
        copy.wait()
    values, sens = y.end_b()
    for k in range(y.step):
        put_slab(work_t, k, y.step, values[k])
        put_slab(other_t, k, y.step, sens[k])
    for layer in range(layers):
        new_heads[layer] = work_t[layer].T
        sens_y[layer] = other_t[layer].T

    for copy in x_b:
        copy.wait()
    values, sens = x.end_b()
    for k in range(x.step):
        put_slab(grad_heads, k, x.step, slab(storage, k, x.step) * values[k])
        put_slab(sens_x, k, x.step, sens[k])


def direction_scratch(count, length, width, layers):
    step = length // BLOCKS
    tile = (layers, BLOCKS, width)
    rows_a = -(-(layers * A + 8) // 8) * 8
    rows_b = -(-(layers * 2) // 8) * 8
    sems = pltpu.SemaphoreType.DMA((max(count - 1, 1),))
    return [
        pltpu.VMEM((step, 3) + tile, jnp.float32),
        pltpu.VMEM((2, step) + tile, jnp.float32),
        pltpu.VMEM((step,) + tile, jnp.float32),
        pltpu.VMEM((step,) + tile, jnp.float32),
        pltpu.VMEM((len(SHIFTS), 6) + tile, jnp.float32),
        pltpu.VMEM((2, len(SHIFTS), 2) + tile, jnp.float32),
        pltpu.VMEM((count, 6, layers, width), jnp.float32),
        pltpu.VMEM((count, rows_b, width), jnp.float32),
        pltpu.VMEM((count, rows_b, width), jnp.float32),
        pltpu.VMEM((count, rows_a, width), jnp.float32),
        pltpu.VMEM((count, rows_b, width), jnp.float32),
        sems, sems, sems, sems,
    ]


def solution(mesh):
    counts = (mesh.shape["gx"], mesh.shape["gy"])

    def on_device(*args):
        layers, rows, columns = args[0].shape
        vmem = pl.BlockSpec(memory_space=pltpu.VMEM)
        smem = pl.BlockSpec(memory_space=pltpu.SMEM)
        natural = pltpu.VMEM((layers, rows, columns), jnp.float32)
        turned = pltpu.VMEM((layers, columns, rows), jnp.float32)
        return pl.pallas_call(
            functools.partial(kernel, counts),
            out_shape=[jax.ShapeDtypeStruct(args[0].shape, jnp.float32)] * 4,
            in_specs=[vmem] * 7 + [smem] * 2,
            out_specs=[vmem] * 4,
            scratch_shapes=[
                pltpu.VMEM((layers, BLOCKS, columns), jnp.float32),
                pltpu.VMEM((rows, columns), jnp.float32),
                pltpu.VMEM((columns, rows), jnp.float32),
                turned, turned, natural, turned, turned,
            ]
            + direction_scratch(counts[0], rows, columns, layers)
            + direction_scratch(counts[1], columns, rows, layers),
            compiler_params=pltpu.CompilerParams(
                collective_id=0, has_side_effects=True, vmem_limit_bytes=40 * 2**20
            ),
        )(*args)

    block = P(None, "gx", "gy")
    return jax.shard_map(
        on_device,
        mesh=mesh,
        in_specs=(block,) * 6 + (P("gx", "gy"), P(), P()),
        out_specs=(block,) * 4,
        check_vma=False,
    )
```

profile of v0, /device:TPU:0, one launch (start us, length us, event | category | flops | bytes accessed | tf_op | source)
XLA Modules:
  0.0 28.1 jit_solution(12812778885911607332)
XLA Ops:
  0.6 0.0 copy-start
  0.6 0.9 %copy-done = f32[4,128,128]{2,1,0:T(8,128)S(1)} copy-done((f32[4,128,128]{2,1,0:T(8,128)S(1)}, f32[4,128,128]{2,1,0:T(8,128)}, u32[]{:S(2)}) %copy-start) | copy-done | bytes 262168
  1.6 0.0 copy-start.1
  1.6 0.9 %copy-done.1 = f32[4,128,128]{2,1,0:T(8,128)S(1)} copy-done((f32[4,128,128]{2,1,0:T(8,128)S(1)}, f32[4,128,128]{2,1,0:T(8,128)}, u32[]{:S(2)}) %copy-start.1) | copy-done | bytes 262168
  2.5 0.0 copy-start.2
  2.5 0.9 %copy-done.2 = f32[4,128,128]{2,1,0:T(8,128)S(1)} copy-done((f32[4,128,128]{2,1,0:T(8,128)S(1)}, f32[4,128,128]{2,1,0:T(8,128)}, u32[]{:S(2)}) %copy-start.2) | copy-done | bytes 262168
  3.5 0.0 copy-start.3
  3.5 0.9 %copy-done.3 = f32[4,128,128]{2,1,0:T(8,128)S(1)} copy-done((f32[4,128,128]{2,1,0:T(8,128)S(1)}, f32[4,128,128]{2,1,0:T(8,128)}, u32[]{:S(2)}) %copy-start.3) | copy-done | bytes 262168
  4.4 0.0 copy-start.4
  4.4 0.9 %copy-done.4 = f32[4,128,128]{2,1,0:T(8,128)S(1)} copy-done((f32[4,128,128]{2,1,0:T(8,128)S(1)}, f32[4,128,128]{2,1,0:T(8,128)}, u32[]{:S(2)}) %copy-start.4) | copy-done | bytes 262168
  5.4 0.0 copy-start.5
  5.4 0.9 %copy-done.5 = f32[4,128,128]{2,1,0:T(8,128)S(1)} copy-done((f32[4,128,128]{2,1,0:T(8,128)S(1)}, f32[4,128,128]{2,1,0:T(8,128)}, u32[]{:S(2)}) %copy-start.5) | copy-done | bytes 262168
  6.3 0.0 copy-start.6
  6.3 0.8 %copy-done.6 = s32[128,128]{1,0:T(8,128)S(1)} copy-done((s32[128,128]{1,0:T(8,128)S(1)}, s32[128,128]{1,0:T(8,128)}, u32[]{:S(2)}) %copy-start.6) | copy-done | bytes 65560
  7.2 0.0 copy-start.7
  7.2 0.7 %copy-done.7 = f32[64]{0:T(128)S(1)} copy-done((f32[64]{0:T(128)S(1)}, f32[64]{0:T(128)}, u32[]{:S(2)}) %copy-start.7) | copy-done | bytes 280
  7.8 0.0 copy-start.8
  7.8 0.7 %copy-done.8 = s32[4]{0:T(128)S(1)} copy-done((s32[4]{0:T(128)S(1)}, s32[4]{0:T(128)}, u32[]{:S(2)}) %copy-start.8) | copy-done | bytes 40
  8.5 16.8 %shard_map.120 = (f32[4,128,128]{2,1,0:T(8,128)S(1)}, f32[4,128,128]{2,1,0:T(8,128)S(1)}, f32[4,128,128]{2,1,0:T(8,128)S(1)}, f32[4,128,128]{2,1,0:T(8,128)S(1)}) custom-call(f32[4,128,128]{2,1,0:T(8,128)S(1)} %copy-done, f32[4,128,128]{2,1,0:T(8,128)S(1)} %copy-done.1, f32[4,128,128]{2,1,0:T(8,128)S(1)} %copy-done.2, f32[4,128,128]{2,1,0:T(8,128)S(1)} %copy-done.3, ...), custom_call_target="tpu_custom_call" | custom-call | tf_op jit(solution)/shard_map/pallas_call | solution.py:360
  25.3 0.7 %copy.17 = f32[4,128,128]{2,1,0:T(8,128)} copy(f32[4,128,128]{2,1,0:T(8,128)S(1)} %get-tuple-element.8) | data formatting | bytes 524288
  26.0 0.7 %copy.18 = f32[4,128,128]{2,1,0:T(8,128)} copy(f32[4,128,128]{2,1,0:T(8,128)S(1)} %get-tuple-element.9) | data formatting | bytes 524288
  26.7 0.7 %copy.19 = f32[4,128,128]{2,1,0:T(8,128)} copy(f32[4,128,128]{2,1,0:T(8,128)S(1)} %get-tuple-element.10) | data formatting | bytes 524288
  27.4 0.7 %copy.20 = f32[4,128,128]{2,1,0:T(8,128)} copy(f32[4,128,128]{2,1,0:T(8,128)S(1)} %get-tuple-element.11) | data formatting | bytes 524288
Async XLA Ops:
  0.6 1.0 %copy-start = (f32[4,128,128]{2,1,0:T(8,128)S(1)}, f32[4,128,128]{2,1,0:T(8,128)}, u32[]{:S(2)}) copy-start(f32[4,128,128]{2,1,0:T(8,128)} %heads.1) | copy-start | bytes 786436
  1.6 0.9 %copy-start.1 = (f32[4,128,128]{2,1,0:T(8,128)S(1)}, f32[4,128,128]{2,1,0:T(8,128)}, u32[]{:S(2)}) copy-start(f32[4,128,128]{2,1,0:T(8,128)} %cond_x.1) | copy-start | bytes 786436
  2.5 0.9 %copy-start.2 = (f32[4,128,128]{2,1,0:T(8,128)S(1)}, f32[4,128,128]{2,1,0:T(8,128)}, u32[]{:S(2)}) copy-start(f32[4,128,128]{2,1,0:T(8,128)} %cond_y.1) | copy-start | bytes 786436
  3.5 0.9 %copy-start.3 = (f32[4,128,128]{2,1,0:T(8,128)S(1)}, f32[4,128,128]{2,1,0:T(8,128)}, u32[]{:S(2)}) copy-start(f32[4,128,128]{2,1,0:T(8,128)} %storage.1) | copy-start | bytes 786436
  4.4 0.9 %copy-start.4 = (f32[4,128,128]{2,1,0:T(8,128)S(1)}, f32[4,128,128]{2,1,0:T(8,128)}, u32[]{:S(2)}) copy-start(f32[4,128,128]{2,1,0:T(8,128)} %sources.1) | copy-start | bytes 786436
  5.4 0.9 %copy-start.5 = (f32[4,128,128]{2,1,0:T(8,128)S(1)}, f32[4,128,128]{2,1,0:T(8,128)}, u32[]{:S(2)}) copy-start(f32[4,128,128]{2,1,0:T(8,128)} %cotangent.1) | copy-start | bytes 786436
  6.3 0.8 %copy-start.6 = (s32[128,128]{1,0:T(8,128)S(1)}, s32[128,128]{1,0:T(8,128)}, u32[]{:S(2)}) copy-start(s32[128,128]{1,0:T(8,128)} %mask.1) | copy-start | bytes 196612
  7.2 0.7 %copy-start.7 = (f32[64]{0:T(128)S(1)}, f32[64]{0:T(128)}, u32[]{:S(2)}) copy-start(f32[64]{0:T(128)} %scale.1) | copy-start | bytes 772
  7.8 0.7 %copy-start.8 = (s32[4]{0:T(128)S(1)}, s32[4]{0:T(128)}, u32[]{:S(2)}) copy-start(s32[4]{0:T(128)} %window.1) | copy-start | bytes 52
where the time goes:
time: 28.5 us; the launch traced here: 28.1 us
  Pallas kernels  16.8 us (59%)
  local copies, waits for them, and re-layouts  10.7 us (38%)
  between operations  0.66 us (2%)
    pallas_call x1, Pallas kernels, on_device(): pl.pallas_call(functools.partial(kernel, counts), out_shape=[jax.ShapeDty...  16.8 us
    unnamed x22, local copies, waits for them, and re-layouts  10.7 us

commit v1 on v0

--- a/solution.py
+++ b/solution.py
@@ -254,9 +254,17 @@
         return x, [self.flux[k] * change[k] for k in range(self.step)]
 
 
-def kernel(counts, heads, cond_x, cond_y, storage, sources, cotangent, mask, scale, window,
-           new_heads, grad_heads, sens_x, sens_y,
-           weight, act, act_t, cond_t, store_t, work, work_t, other_t, *rest):
+def kernel(counts, *refs):
+    sources_hbm, refs = refs[:9], refs[9:]
+    results, refs = refs[:4], refs[4:]
+    (new_heads, grad_heads, sens_x, sens_y), leave, refs = refs[:4], refs[4], refs[5:]
+    stores = [
+        pltpu.make_async_copy(src, dst, leave.at[at])
+        for at, (src, dst) in enumerate(zip((new_heads, grad_heads, sens_x, sens_y), results))
+    ]
+    copied, refs = refs[:9], refs[9:]
+    heads, cond_x, cond_y, storage, sources, cotangent, mask, scale, window = copied
+    (arrive, weight, act, act_t, cond_t, store_t, work, work_t, other_t), rest = refs[:9], refs[9:]
     layers, rows, columns = heads.shape
     half = len(rest) // 2
     x = Direction("gx", counts[0], rows, layers, rest[:half])
@@ -264,26 +272,36 @@
     barrier = pltpu.get_barrier_semaphore()
     x.greet(barrier)
     y.greet(barrier)
-
+    loads = [pltpu.make_async_copy(src, dst, arrive.at[at]) for at, (src, dst) in enumerate(zip(sources_hbm, copied))]
+    for at in (8, 7, 6, 1, 3, 0, 4, 2, 5):
+        loads[at].start()
+
+    loads[8].wait()
+    loads[7].wait()
     for layer in range(layers):
         weight[layer] = jnp.full(weight.shape[1:], scale[window[layer]], jnp.float32)
+    loads[6].wait()
     act[...] = mask[...].astype(jnp.float32)
     act_t[...] = act[...].T
+    for at in (1, 3, 0, 4):
+        loads[at].wait()
+
+    x.begin_a(cond_x, storage, act, weight,
+              lambda k: slab(storage, k, x.step) * slab(heads, k, x.step) + slab(sources, k, x.step))
+    pl.semaphore_wait(barrier, counts[0] + counts[1] - 2)
+    x_a = x.copies(x.buf_a, x.send_a, x.recv_a)
+    for copy in x_a:
+        copy.start()
+
+    loads[2].wait()
+    loads[5].wait()
     for layer in range(layers):
         cond_t[layer] = cond_y[layer].T
         store_t[layer] = storage[layer].T
         work_t[layer] = cotangent[layer].T
-
     y.begin_a(cond_t, store_t, act_t, weight, lambda k: slab(work_t, k, y.step))
-    pl.semaphore_wait(barrier, counts[0] + counts[1] - 2)
     y_a = y.copies(y.buf_a, y.send_a, y.recv_a)
     for copy in y_a:
-        copy.start()
-
-    x.begin_a(cond_x, storage, act, weight,
-              lambda k: slab(storage, k, x.step) * slab(heads, k, x.step) + slab(sources, k, x.step))
-    x_a = x.copies(x.buf_a, x.send_a, x.recv_a)
-    for copy in x_a:
         copy.start()
 
     for copy in x_a:
@@ -293,12 +311,12 @@
     for layer in range(layers):
         work_t[layer] = work[layer].T
     y.begin_b(lambda k: slab(work_t, k, y.step))
-
-    for copy in y_a:
-        copy.wait()
     y_b = y.copies(y.buf_b, y.send_b, y.recv_b)
     for copy in y_b:
         copy.start()
+
+    for copy in y_a:
+        copy.wait()
     for k, value in enumerate(y.end_a()):
         put_slab(other_t, k, y.step, slab(store_t, k, y.step) * value)
     for layer in range(layers):
@@ -317,6 +335,8 @@
     for layer in range(layers):
         new_heads[layer] = work_t[layer].T
         sens_y[layer] = other_t[layer].T
+    stores[0].start()
+    stores[3].start()
 
     for copy in x_b:
         copy.wait()
@@ -324,6 +344,19 @@
     for k in range(x.step):
         put_slab(grad_heads, k, x.step, slab(storage, k, x.step) * values[k])
         put_slab(sens_x, k, x.step, sens[k])
+    stores[1].start()
+    stores[2].start()
+    for copy in stores:
+        copy.wait()
+
+
+def write_out(*refs):
+    count = len(refs) // 2
+    copies = [pltpu.make_async_copy(refs[i], refs[count + i], refs[-1].at[i]) for i in range(count)]
+    for copy in copies:
+        copy.start()
+    for copy in copies:
+        copy.wait()
 
 
 def direction_scratch(count, length, width, layers):
@@ -353,16 +386,21 @@
 
     def on_device(*args):
         layers, rows, columns = args[0].shape
-        vmem = pl.BlockSpec(memory_space=pltpu.VMEM)
-        smem = pl.BlockSpec(memory_space=pltpu.SMEM)
+        hbm = pl.BlockSpec(memory_space=pltpu.HBM)
         natural = pltpu.VMEM((layers, rows, columns), jnp.float32)
         turned = pltpu.VMEM((layers, columns, rows), jnp.float32)
-        return pl.pallas_call(
+        results = [jax.ShapeDtypeStruct(args[0].shape, jnp.float32)] * 4
+        found = pl.pallas_call(
             functools.partial(kernel, counts),
-            out_shape=[jax.ShapeDtypeStruct(args[0].shape, jnp.float32)] * 4,
-            in_specs=[vmem] * 7 + [smem] * 2,
-            out_specs=[vmem] * 4,
-            scratch_shapes=[
+            out_shape=results,
+            in_specs=[hbm] * 9,
+            out_specs=[hbm] * 4,
+            scratch_shapes=[natural] * 4
+            + [pltpu.SemaphoreType.DMA((4,))]
+            + [pltpu.VMEM(v.shape, v.dtype) for v in args[:7]]
+            + [pltpu.SMEM(v.shape, v.dtype) for v in args[7:]]
+            + [
+                pltpu.SemaphoreType.DMA((9,)),
                 pltpu.VMEM((layers, BLOCKS, columns), jnp.float32),
                 pltpu.VMEM((rows, columns), jnp.float32),
                 pltpu.VMEM((columns, rows), jnp.float32),
@@ -371,9 +409,17 @@
             + direction_scratch(counts[0], rows, columns, layers)
             + direction_scratch(counts[1], columns, rows, layers),
             compiler_params=pltpu.CompilerParams(
-                collective_id=0, has_side_effects=True, vmem_limit_bytes=40 * 2**20
+                collective_id=0, has_side_effects=True, vmem_limit_bytes=64 * 2**20
             ),
         )(*args)
+        return pl.pallas_call(
+            write_out,
+            out_shape=results,
+            in_specs=[hbm] * 4,
+            out_specs=[hbm] * 4,
+            scratch_shapes=[pltpu.SemaphoreType.DMA((4,))],
+            compiler_params=pltpu.CompilerParams(vmem_limit_bytes=64 * 2**20),
+        )(*found)
 
     block = P(None, "gx", "gy")
     return jax.shard_map(

time: 28.5 us -> 49.1 us (1.72)
  Pallas kernels: 16.8 us -> 48.4 us
  local copies, waits for them, and re-layouts: 10.7 us -> 0 us
    pallas_call x1 -> x2, Pallas kernels: 16.8 us -> 48.4 us  [the longest x1 32.9 us: on_device(): pl.pallas_call(write_out, out_shape=results, in_specs=[hbm] * 4, out_spec...]
    unnamed x22 -> x0, local copies, waits for them, and re-layouts: 10.7 us -> none
where the time goes in v1:
time: 49.1 us; the launch traced here: 49 us
  Pallas kernels  48.4 us (99%)
  between operations  0.64 us (1%)
    pallas_call x1, Pallas kernels, on_device(): pl.pallas_call(write_out, out_shape=results, in_specs=[hbm] * 4, out_spec...  32.9 us
    pallas_call x1, Pallas kernels, on_device(): pl.pallas_call(functools.partial(kernel, counts), out_shape=results, in_s...  15.5 us

profile of v1, /device:TPU:0, one launch (start us, length us, event | category | flops | bytes accessed | tf_op | source)
XLA Modules:
  0.0 49.0 jit_solution(14081772731785138516)
XLA Ops:
  0.6 15.5 %shard_map.120 = (f32[4,128,128]{2,1,0:T(8,128)}, f32[4,128,128]{2,1,0:T(8,128)}, f32[4,128,128]{2,1,0:T(8,128)}, f32[4,128,128]{2,1,0:T(8,128)}) custom-call(f32[4,128,128]{2,1,0:T(8,128)} %refs_0_.1, f32[4,128,128]{2,1,0:T(8,128)} %refs_1_.1, f32[4,128,128]{2,1,0:T(8,128)} %refs_2_.1, f32[4,128,128]{2,1,0:T(8,128)} %refs_3_.1, f32[4,128,128]{2,1,0:T(8,128)} %refs_4_.1, ...), custom_call_target="tpu_custom_call" | custom-call | tf_op jit(solution)/shard_map/pallas_call | solution.py:393
  16.1 32.9 %shard_map.121 = (f32[4,128,128]{2,1,0:T(8,128)}, f32[4,128,128]{2,1,0:T(8,128)}, f32[4,128,128]{2,1,0:T(8,128)}, f32[4,128,128]{2,1,0:T(8,128)}) custom-call(f32[4,128,128]{2,1,0:T(8,128)} %get-tuple-element.8.refs_0_, f32[4,128,128]{2,1,0:T(8,128)} %get-tuple-element.9.refs_1_, f32[4,128,128]{2,1,0:T(8,128)} %get-tuple-element.10.refs_2_, ...), custom_call_target="tpu_custom_call" | custom-call | tf_op jit(solution)/shard_map/pallas_call | solution.py:415

commit v2 on v1

--- a/solution.py
+++ b/solution.py
@@ -256,12 +256,7 @@
 
 def kernel(counts, *refs):
     sources_hbm, refs = refs[:9], refs[9:]
-    results, refs = refs[:4], refs[4:]
-    (new_heads, grad_heads, sens_x, sens_y), leave, refs = refs[:4], refs[4], refs[5:]
-    stores = [
-        pltpu.make_async_copy(src, dst, leave.at[at])
-        for at, (src, dst) in enumerate(zip((new_heads, grad_heads, sens_x, sens_y), results))
-    ]
+    (new_heads, grad_heads, sens_x, sens_y), refs = refs[:4], refs[4:]
     copied, refs = refs[:9], refs[9:]
     heads, cond_x, cond_y, storage, sources, cotangent, mask, scale, window = copied
     (arrive, weight, act, act_t, cond_t, store_t, work, work_t, other_t), rest = refs[:9], refs[9:]
@@ -335,8 +330,6 @@
     for layer in range(layers):
         new_heads[layer] = work_t[layer].T
         sens_y[layer] = other_t[layer].T
-    stores[0].start()
-    stores[3].start()
 
     for copy in x_b:
         copy.wait()
@@ -344,10 +337,6 @@
     for k in range(x.step):
         put_slab(grad_heads, k, x.step, slab(storage, k, x.step) * values[k])
         put_slab(sens_x, k, x.step, sens[k])
-    stores[1].start()
-    stores[2].start()
-    for copy in stores:
-        copy.wait()
 
 
 def write_out(*refs):
@@ -386,18 +375,17 @@
 
     def on_device(*args):
         layers, rows, columns = args[0].shape
+        vmem = pl.BlockSpec(memory_space=pltpu.VMEM)
         hbm = pl.BlockSpec(memory_space=pltpu.HBM)
         natural = pltpu.VMEM((layers, rows, columns), jnp.float32)
         turned = pltpu.VMEM((layers, columns, rows), jnp.float32)
         results = [jax.ShapeDtypeStruct(args[0].shape, jnp.float32)] * 4
         found = pl.pallas_call(
             functools.partial(kernel, counts),
-            out_shape=results,
+            out_shape=[pltpu.VMEM(args[0].shape, jnp.float32)] * 4,
             in_specs=[hbm] * 9,
-            out_specs=[hbm] * 4,
-            scratch_shapes=[natural] * 4
-            + [pltpu.SemaphoreType.DMA((4,))]
-            + [pltpu.VMEM(v.shape, v.dtype) for v in args[:7]]
+            out_specs=[vmem] * 4,
+            scratch_shapes=[pltpu.VMEM(v.shape, v.dtype) for v in args[:7]]
             + [pltpu.SMEM(v.shape, v.dtype) for v in args[7:]]
             + [
                 pltpu.SemaphoreType.DMA((9,)),
@@ -409,16 +397,15 @@
             + direction_scratch(counts[0], rows, columns, layers)
             + direction_scratch(counts[1], columns, rows, layers),
             compiler_params=pltpu.CompilerParams(
-                collective_id=0, has_side_effects=True, vmem_limit_bytes=64 * 2**20
+                collective_id=0, has_side_effects=True, vmem_limit_bytes=40 * 2**20
             ),
-        )(*args)
+        )(*[pltpu.with_memory_space_constraint(v, pltpu.HBM) for v in args])
         return pl.pallas_call(
             write_out,
             out_shape=results,
-            in_specs=[hbm] * 4,
+            in_specs=[vmem] * 4,
             out_specs=[hbm] * 4,
             scratch_shapes=[pltpu.SemaphoreType.DMA((4,))],
-            compiler_params=pltpu.CompilerParams(vmem_limit_bytes=64 * 2**20),
         )(*found)
 
     block = P(None, "gx", "gy")

time: 49.1 us -> 20.4 us (0.42)
  Pallas kernels: 48.4 us -> 16.8 us
  local copies, waits for them, and re-layouts: 0 us -> 2.78 us
    pallas_call x2, Pallas kernels: 48.4 us -> 16.8 us  [the longest x1 14.6 us: on_device(): pl.pallas_call(functools.partial(kernel, counts), out_shape=[pltpu.VMEM(a...]
    unnamed x0 -> x8, local copies, waits for them, and re-layouts: none -> 2.78 us
where the time goes in v2:
time: 20.4 us; the launch traced here: 20.2 us
  Pallas kernels  16.8 us (82%)
  local copies, waits for them, and re-layouts  2.78 us (14%)
  between operations  0.65 us (3%)
    pallas_call x1, Pallas kernels, on_device(): pl.pallas_call(functools.partial(kernel, counts), out_shape=[pltpu.VMEM(a...  14.6 us
    unnamed x8, local copies, waits for them, and re-layouts  2.78 us
    pallas_call x1, Pallas kernels, on_device(): pl.pallas_call(write_out, out_shape=results, in_specs=[vmem] * 4, out_spe...  2.18 us

profile of v2, /device:TPU:0, one launch (start us, length us, event | category | flops | bytes accessed | tf_op | source)
XLA Modules:
  0.0 20.2 jit_solution(12152644810604279815)
XLA Ops:
  0.6 14.6 %shard_map.120 = (f32[4,128,128]{2,1,0:T(8,128)S(1)}, f32[4,128,128]{2,1,0:T(8,128)S(1)}, f32[4,128,128]{2,1,0:T(8,128)S(1)}, f32[4,128,128]{2,1,0:T(8,128)S(1)}) custom-call(f32[4,128,128]{2,1,0:T(8,128)} %refs_0_.1, f32[4,128,128]{2,1,0:T(8,128)} %refs_1_.1, f32[4,128,128]{2,1,0:T(8,128)} %refs_2_.1, f32[4,128,128]{2,1,0:T(8,128)} %refs_3_.1, ...), custom_call_target="tpu_custom_call" | custom-call | tf_op jit(solution)/shard_map/pallas_call | solution.py:383
  15.3 0.0 copy-start
  15.3 0.7 %copy-done = f32[4,128,128]{2,1,0:T(8,128)} copy-done((f32[4,128,128]{2,1,0:T(8,128)}, f32[4,128,128]{2,1,0:T(8,128)S(1)}, u32[]{:S(2)}) %copy-start) | copy-done | bytes 262168
  16.0 0.0 copy-start.1
  16.0 0.7 %copy-done.1 = f32[4,128,128]{2,1,0:T(8,128)} copy-done((f32[4,128,128]{2,1,0:T(8,128)}, f32[4,128,128]{2,1,0:T(8,128)S(1)}, u32[]{:S(2)}) %copy-start.1) | copy-done | bytes 262168
  16.7 0.0 copy-start.2
  16.7 0.7 %copy-done.2 = f32[4,128,128]{2,1,0:T(8,128)} copy-done((f32[4,128,128]{2,1,0:T(8,128)}, f32[4,128,128]{2,1,0:T(8,128)S(1)}, u32[]{:S(2)}) %copy-start.2) | copy-done | bytes 262168
  17.4 0.0 copy-start.3
  17.4 0.7 %copy-done.3 = f32[4,128,128]{2,1,0:T(8,128)} copy-done((f32[4,128,128]{2,1,0:T(8,128)}, f32[4,128,128]{2,1,0:T(8,128)S(1)}, u32[]{:S(2)}) %copy-start.3) | copy-done | bytes 262168
  18.1 2.2 %shard_map.121 = (f32[4,128,128]{2,1,0:T(8,128)}, f32[4,128,128]{2,1,0:T(8,128)}, f32[4,128,128]{2,1,0:T(8,128)}, f32[4,128,128]{2,1,0:T(8,128)}) custom-call(f32[4,128,128]{2,1,0:T(8,128)} %copy-done, f32[4,128,128]{2,1,0:T(8,128)} %copy-done.1, f32[4,128,128]{2,1,0:T(8,128)} %copy-done.2, f32[4,128,128]{2,1,0:T(8,128)} %copy-done.3), custom_call_target="tpu_custom_call" | custom-call | tf_op jit(solution)/shard_map/pallas_call | solution.py:403
Async XLA Ops:
  15.3 0.7 %copy-start = (f32[4,128,128]{2,1,0:T(8,128)}, f32[4,128,128]{2,1,0:T(8,128)S(1)}, u32[]{:S(2)}) copy-start(f32[4,128,128]{2,1,0:T(8,128)S(1)} %get-tuple-element.8.refs_0_) | copy-start | bytes 786436
  16.0 0.7 %copy-start.1 = (f32[4,128,128]{2,1,0:T(8,128)}, f32[4,128,128]{2,1,0:T(8,128)S(1)}, u32[]{:S(2)}) copy-start(f32[4,128,128]{2,1,0:T(8,128)S(1)} %get-tuple-element.9.refs_1_) | copy-start | bytes 786436
  16.7 0.7 %copy-start.2 = (f32[4,128,128]{2,1,0:T(8,128)}, f32[4,128,128]{2,1,0:T(8,128)S(1)}, u32[]{:S(2)}) copy-start(f32[4,128,128]{2,1,0:T(8,128)S(1)} %get-tuple-element.10.refs_2_) | copy-start | bytes 786436
  17.4 0.7 %copy-start.3 = (f32[4,128,128]{2,1,0:T(8,128)}, f32[4,128,128]{2,1,0:T(8,128)S(1)}, u32[]{:S(2)}) copy-start(f32[4,128,128]{2,1,0:T(8,128)S(1)} %get-tuple-element.11.refs_3_) | copy-start | bytes 786436

commit v3 on v2

--- a/solution.py
+++ b/solution.py
@@ -73,7 +73,7 @@
 class Direction:
     def __init__(self, axis, count, length, layers, refs):
         self.axis, self.count, self.step, self.layers = axis, count, length // BLOCKS, layers
-        (self.coef, self.part, self.face, self.flux, self.bcoef, self.bpart, self.dcoef, self.dx, self.ends,
+        (self.coef, self.part, self.face, self.flux, self.store, self.bcoef, self.bpart, self.dcoef, self.dx, self.ends,
          self.buf_a, self.buf_b, self.send_a, self.recv_a, self.send_b, self.recv_b) = refs
         self.me = lax.axis_index(axis)
         self.order = schedule(self.step)
@@ -120,7 +120,9 @@
         act = [active[pl.ds(k, BLOCKS, stride=step), :] for k in range(step)]
         weight = weight[...]
         store = [slab(storage, k, step) for k in range(step)]
-        right = [right_of(k) for k in range(step)]
+        for k in range(step):
+            self.store[k] = store[k]
+        right = [right_of(k, store[k]) for k in range(step)]
         face = []
         for k in range(step):
             raw = jnp.exp(slab(cond, k, step)) * weight * act[k][None]
@@ -282,7 +284,7 @@
         loads[at].wait()
 
     x.begin_a(cond_x, storage, act, weight,
-              lambda k: slab(storage, k, x.step) * slab(heads, k, x.step) + slab(sources, k, x.step))
+              lambda k, store: store * slab(heads, k, x.step) + slab(sources, k, x.step))
     pl.semaphore_wait(barrier, counts[0] + counts[1] - 2)
     x_a = x.copies(x.buf_a, x.send_a, x.recv_a)
     for copy in x_a:
@@ -294,15 +296,15 @@
         cond_t[layer] = cond_y[layer].T
         store_t[layer] = storage[layer].T
         work_t[layer] = cotangent[layer].T
-    y.begin_a(cond_t, store_t, act_t, weight, lambda k: slab(work_t, k, y.step))
+    y.begin_a(cond_t, store_t, act_t, weight, lambda k, store: slab(work_t, k, y.step))
     y_a = y.copies(y.buf_a, y.send_a, y.recv_a)
     for copy in y_a:
         copy.start()
 
     for copy in x_a:
-        copy.wait()
+        copy.wait_recv()
     for k, value in enumerate(x.end_a()):
-        put_slab(work, k, x.step, slab(storage, k, x.step) * value)
+        put_slab(work, k, x.step, x.store[k] * value)
     for layer in range(layers):
         work_t[layer] = work[layer].T
     y.begin_b(lambda k: slab(work_t, k, y.step))
@@ -311,9 +313,9 @@
         copy.start()
 
     for copy in y_a:
-        copy.wait()
+        copy.wait_recv()
     for k, value in enumerate(y.end_a()):
-        put_slab(other_t, k, y.step, slab(store_t, k, y.step) * value)
+        put_slab(other_t, k, y.step, y.store[k] * value)
     for layer in range(layers):
         work[layer] = other_t[layer].T
     x.begin_b(lambda k: slab(work, k, x.step))
@@ -322,7 +324,7 @@
         copy.start()
 
     for copy in y_b:
-        copy.wait()
+        copy.wait_recv()
     values, sens = y.end_b()
     for k in range(y.step):
         put_slab(work_t, k, y.step, values[k])
@@ -332,11 +334,13 @@
         sens_y[layer] = other_t[layer].T
 
     for copy in x_b:
-        copy.wait()
+        copy.wait_recv()
     values, sens = x.end_b()
     for k in range(x.step):
-        put_slab(grad_heads, k, x.step, slab(storage, k, x.step) * values[k])
+        put_slab(grad_heads, k, x.step, x.store[k] * values[k])
         put_slab(sens_x, k, x.step, sens[k])
+    for copy in x_a + y_a + x_b + y_b:
+        copy.wait_send()
 
 
 def write_out(*refs):
@@ -357,6 +361,7 @@
     return [
         pltpu.VMEM((step, 3) + tile, jnp.float32),
         pltpu.VMEM((2, step) + tile, jnp.float32),
+        pltpu.VMEM((step,) + tile, jnp.float32),
         pltpu.VMEM((step,) + tile, jnp.float32),
         pltpu.VMEM((step,) + tile, jnp.float32),
         pltpu.VMEM((len(SHIFTS), 6) + tile, jnp.float32),
@@ -406,7 +411,8 @@
             in_specs=[vmem] * 4,
             out_specs=[hbm] * 4,
             scratch_shapes=[pltpu.SemaphoreType.DMA((4,))],
-        )(*found)
+            compiler_params=pltpu.CompilerParams(vmem_limit_bytes=2 * 2**20),
+        )(*[pltpu.with_memory_space_constraint(v, pltpu.VMEM) for v in found])
 
     block = P(None, "gx", "gy")
     return jax.shard_map(

time: 20.4 us -> 16.4 us (0.80)
  local copies, waits for them, and re-layouts: 2.78 us -> 0 us
  Pallas kernels: 16.8 us -> 15.6 us
    unnamed x8 -> x0, local copies, waits for them, and re-layouts: 2.78 us -> none
    pallas_call x1, Pallas kernels: 2.18 us -> 1 us  [on_device(): pl.pallas_call(write_out, out_shape=results, in_specs=[vmem] * 4, out_spe...]
where the time goes in v3:
time: 16.4 us; the launch traced here: 16.2 us
  Pallas kernels  15.6 us (95%)
  between operations  0.64 us (4%)
    pallas_call x1, Pallas kernels, on_device(): pl.pallas_call(functools.partial(kernel, counts), out_shape=[pltpu.VMEM(a...  14.6 us
    pallas_call x1, Pallas kernels, on_device(): pl.pallas_call(write_out, out_shape=results, in_specs=[vmem] * 4, out_spe...  1 us

profile of v3, /device:TPU:0, one launch (start us, length us, event | category | flops | bytes accessed | tf_op | source)
XLA Modules:
  0.0 16.2 jit_solution(694838076555889372)
XLA Ops:
  0.6 14.6 %shard_map.120 = (f32[4,128,128]{2,1,0:T(8,128)S(1)}, f32[4,128,128]{2,1,0:T(8,128)S(1)}, f32[4,128,128]{2,1,0:T(8,128)S(1)}, f32[4,128,128]{2,1,0:T(8,128)S(1)}) custom-call(f32[4,128,128]{2,1,0:T(8,128)} %refs_0_.1, f32[4,128,128]{2,1,0:T(8,128)} %refs_1_.1, f32[4,128,128]{2,1,0:T(8,128)} %refs_2_.1, f32[4,128,128]{2,1,0:T(8,128)} %refs_3_.1, ...), custom_call_target="tpu_custom_call" | custom-call | tf_op jit(solution)/shard_map/pallas_call | solution.py:388
  15.2 1.0 %shard_map.121 = (f32[4,128,128]{2,1,0:T(8,128)}, f32[4,128,128]{2,1,0:T(8,128)}, f32[4,128,128]{2,1,0:T(8,128)}, f32[4,128,128]{2,1,0:T(8,128)}) custom-call(f32[4,128,128]{2,1,0:T(8,128)S(1)} %get-tuple-element.8.refs_0_, f32[4,128,128]{2,1,0:T(8,128)S(1)} %get-tuple-element.9.refs_1_, f32[4,128,128]{2,1,0:T(8,128)S(1)} %get-tuple-element.10.refs_2_, ...), custom_call_target="tpu_custom_call" | custom-call | tf_op jit(solution)/shard_map/pallas_call | solution.py:408

commit v4 on v3

--- a/solution.py
+++ b/solution.py
@@ -26,7 +26,7 @@
 
 
 def weights(fl, fr, s):
-    inv = 1.0 / (fl + fr + s)
+    inv = pl.reciprocal(fl + fr + s)
     return fl * inv, fr * inv, inv
 
 
@@ -180,9 +180,9 @@
                 links.append(faces[-1])
             segs, faces = joined, links
         g1, g2, t = segs[0]
-        inv = 1.0 / (t + g2)
+        inv = pl.reciprocal(t + g2)
         w = t * inv
-        self.dcoef[slot, 0], self.dcoef[slot, 1], self.dcoef[slot, 2] = w, inv, 1.0 / (g1 + w * g2)
+        self.dcoef[slot, 0], self.dcoef[slot, 1], self.dcoef[slot, 2] = w, inv, pl.reciprocal(g1 + w * g2)
 
     def solve_devices(self, pairs):
         slot, tree = 0, []

time: 16.4 us -> 16.4 us (level)
  no operation moved by 1% of the time
where the time goes in v4:
time: 16.4 us; the launch traced here: 16.2 us
  Pallas kernels  15.6 us (95%)
  between operations  0.64 us (4%)
    pallas_call x1, Pallas kernels, on_device(): pl.pallas_call(functools.partial(kernel, counts), out_shape=[pltpu.VMEM(a...  14.6 us
    pallas_call x1, Pallas kernels, on_device(): pl.pallas_call(write_out, out_shape=results, in_specs=[vmem] * 4, out_spe...  1 us

profile of v4, /device:TPU:0, one launch (start us, length us, event | category | flops | bytes accessed | tf_op | source)
XLA Modules:
  0.0 16.2 jit_solution(694838076555889372)
XLA Ops:
  0.6 14.6 %shard_map.120 = (f32[4,128,128]{2,1,0:T(8,128)S(1)}, f32[4,128,128]{2,1,0:T(8,128)S(1)}, f32[4,128,128]{2,1,0:T(8,128)S(1)}, f32[4,128,128]{2,1,0:T(8,128)S(1)}) custom-call(f32[4,128,128]{2,1,0:T(8,128)} %refs_0_.1, f32[4,128,128]{2,1,0:T(8,128)} %refs_1_.1, f32[4,128,128]{2,1,0:T(8,128)} %refs_2_.1, f32[4,128,128]{2,1,0:T(8,128)} %refs_3_.1, ...), custom_call_target="tpu_custom_call" | custom-call | tf_op jit(solution)/shard_map/pallas_call | solution.py:388
  15.2 1.0 %shard_map.121 = (f32[4,128,128]{2,1,0:T(8,128)}, f32[4,128,128]{2,1,0:T(8,128)}, f32[4,128,128]{2,1,0:T(8,128)}, f32[4,128,128]{2,1,0:T(8,128)}) custom-call(f32[4,128,128]{2,1,0:T(8,128)S(1)} %get-tuple-element.8.refs_0_, f32[4,128,128]{2,1,0:T(8,128)S(1)} %get-tuple-element.9.refs_1_, f32[4,128,128]{2,1,0:T(8,128)S(1)} %get-tuple-element.10.refs_2_, ...), custom_call_target="tpu_custom_call" | custom-call | tf_op jit(solution)/shard_map/pallas_call | solution.py:408
